TPU v7x, 32 devices: a whole 2x2x4 slice. The times are simulated.
32 devices in a mesh: tok: 8 (over z, y), head: 4 (over x, core).
Axes of the slice: x: 2, y: 2, z: 4, core: 2. Of those that a mesh axis runs over, the one named last changes fastest.
Arguments:
- queries: bfloat16 [2048, 24, 128], P('tok', 'head'), may hold values from -4.5 to 4.5
- keys: bfloat16 [2048, 24, 128], P('tok', 'head'), may hold values from -4.5 to 4.5
- values: bfloat16 [2048, 24, 128], P('tok', 'head'), may hold values from -5 to 5
- grad_out: bfloat16 [2048, 3072], P('tok', 'head'), may hold values from -6 to 6
- w_out: bfloat16 [3072, 3072], P('head'), may hold values from -0.109375 to 0.109375
- crit: int32 [8, 40], P('tok'), may hold values from -1 to 127, as said below
Outputs:
- grad_q: bfloat16 [2048, 24, 128], P('tok', 'head')
- grad_k: bfloat16 [2048, 24, 128], P('tok', 'head')
- grad_v: bfloat16 [2048, 24, 128], P('tok', 'head')
Inputs may be any that keep to these rules, and one draw needn't show every extreme that they name: `crit`: row b lists distinct key tiles, -1 marking unused entries, which come last; no listed tile lies in query block b - 1, b or b + 1 (not counted round); at most 8 tiles of one row lie in one query block, and some row has 8 tiles in one block; row 0 lists a tile of block 7 and row 7 a tile of block 0; some row has no unused entry, and every row uses half of its entries or more.
All inputs are finite; a program needn't handle non-finite values.
Results may differ from a plain program's by a relative error of at most 0.022.
Values may be sent and summed in bfloat16 or wider, within the bound.
A program may use at most 128 MiB of HBM per device.

v0:
```python
import jax
import jax.numpy as jnp
from jax import lax
from jax.sharding import PartitionSpec as P

KT = 16


def padded(cells, sides, width):
    for axis, dim in sides:
        count = lax.axis_size(axis)
        ends = count - 1
        head = lax.slice_in_dim(cells, 0, width, axis=dim)
        tail = lax.slice_in_dim(cells, cells.shape[dim] - width, cells.shape[dim], axis=dim)
        cells = jnp.concatenate(
            [
                lax.ppermute(tail, axis, [(i, (i + 1) % count) for i in range(ends)]),
                cells,
                lax.ppermute(head, axis, [((i + 1) % count, i) for i in range(ends)]),
            ],
            axis=dim,
        )
    return cells


def shifted(value, axis, steps):
    count = lax.axis_size(axis)
    leading, last = (max(0, -steps), min(count, count - steps))
    return lax.ppermute(value, axis, [(source, source + steps) for source in range(leading, last)])


def shards(queries, keys, values, grad_out, w_out, crit):
    tok_rows, heads_here, head_dim = queries.shape
    width_here = heads_here * head_dim
    count = lax.axis_size("tok")
    place = lax.axis_index("tok")
    tiles_here = tok_rows // KT
    ncrit = crit.shape[1]
    capacity = (ncrit + count - 4) // (count - 3)
    slots = count * capacity
    row_len = KT * width_here
    d_attn = lax.dot_general(
        lax.all_gather(grad_out, "head", axis=1, tiled=True),
        w_out,
        (((1,), (1,)), ((), ())),
        preferred_element_type=jnp.float32,
    )
    d_attn = d_attn.astype(jnp.bfloat16).reshape(tok_rows, heads_here, head_dim)
    tiles = crit[0]
    used = tiles >= 0
    owner = jnp.where(used, tiles // tiles_here, -1)
    local_tile = jnp.where(used, tiles % tiles_here, 0)
    order = jnp.arange(ncrit)
    earlier = (owner[:, None] == owner[None, :]) & (order[:, None] > order[None, :]) & used[None, :]
    slot = jnp.sum(earlier.astype(jnp.int32), axis=1)
    position = jnp.where(used, owner * capacity + slot, 0)
    slot_ids = jnp.arange(slots)
    chosen = used[:, None] & (position[:, None] == slot_ids[None, :])
    request = jnp.sum(jnp.where(chosen, local_tile[:, None] + 1, 0), axis=0) - 1
    has_left = place > 0
    has_right = place < count - 1
    asked = lax.all_to_all(
        request.reshape(count, capacity), "tok", split_axis=0, concat_axis=0, tiled=True
    ).reshape(slots)
    pair = jnp.stack([keys, values])
    pair_tiles = pair.reshape(2, tiles_here, KT, heads_here, head_dim)
    served = jnp.take(pair_tiles, jnp.clip(asked, 0, tiles_here - 1), axis=1)
    served = jnp.where((asked >= 0)[None, :, None, None, None], served, jnp.zeros((), jnp.bfloat16))
    fetched = lax.all_to_all(
        served.reshape(2, count, capacity, KT, heads_here, head_dim),
        "tok",
        split_axis=1,
        concat_axis=1,
        tiled=True,
    )
    fetched = fetched.reshape(2, slots, KT, heads_here, head_dim)
    far_pair = jnp.take(fetched, position, axis=1).reshape(2, ncrit * KT, heads_here, head_dim)
    window = padded(pair, (("tok", 1),), KT)
    key_pair = jnp.concatenate([window, far_pair], axis=1)
    valid = jnp.concatenate(
        [
            jnp.broadcast_to(has_left, (KT,)),
            jnp.ones((tok_rows,), bool),
            jnp.broadcast_to(has_right, (KT,)),
            jnp.repeat(used, KT),
        ]
    )
    scale = head_dim ** (-0.5)
    key_all = key_pair[0]
    value_all = key_pair[1]
    scores = (
        jnp.einsum("qhd,khd->hqk", queries, key_all, preferred_element_type=jnp.float32) * scale
    )
    scores = jnp.where(valid[None, None, :], scores, -1e30)
    top = jnp.max(scores, axis=-1, keepdims=True)
    probs = jnp.exp(scores - top)
    probs = probs / jnp.sum(probs, axis=-1, keepdims=True)
    probs_b = probs.astype(jnp.bfloat16)
    dprob = jnp.einsum("qhd,khd->hqk", d_attn, value_all, preferred_element_type=jnp.float32)
    delta = jnp.sum(probs * dprob, axis=-1, keepdims=True)
    dscore = (probs * (dprob - delta) * scale).astype(jnp.bfloat16)
    grad_q = jnp.einsum("hqk,khd->qhd", dscore, key_all, preferred_element_type=jnp.float32).astype(
        jnp.bfloat16
    )
    part_k = jnp.einsum("hqk,qhd->khd", dscore, queries, preferred_element_type=jnp.float32)
    part_v = jnp.einsum("hqk,qhd->khd", probs_b, d_attn, preferred_element_type=jnp.float32)
    grads = jnp.stack([part_k, part_v]) * valid.astype(jnp.float32)[None, :, None, None]
    left_part = grads[:, :KT]
    own_part = grads[:, KT : KT + tok_rows]
    right_part = grads[:, KT + tok_rows : 2 * KT + tok_rows]
    far_part = grads[:, 2 * KT + tok_rows :].reshape(2, ncrit, row_len)
    slotted = jnp.einsum(
        "cs,ecr->esr", chosen.astype(jnp.float32), far_part, precision=lax.Precision.HIGHEST
    )
    returned = lax.all_to_all(
        slotted.reshape(2, count, capacity, row_len).astype(jnp.bfloat16),
        "tok",
        split_axis=1,
        concat_axis=1,
        tiled=True,
    ).astype(jnp.float32)
    returned = returned.reshape(2, slots, row_len)
    owned = (asked[None, :] == jnp.arange(tiles_here)[:, None]).astype(jnp.float32)
    added = jnp.einsum("ts,esr->etr", owned, returned, precision=lax.Precision.HIGHEST)
    total = own_part + added.reshape(2, tok_rows, heads_here, head_dim)
    from_next = shifted(left_part.astype(jnp.bfloat16), "tok", -1).astype(left_part.dtype)
    from_prev = shifted(right_part.astype(jnp.bfloat16), "tok", 1).astype(right_part.dtype)
    total = total + jnp.pad(from_next, ((0, 0), (tok_rows - KT, 0), (0, 0), (0, 0)))
    total = total + jnp.pad(from_prev, ((0, 0), (0, tok_rows - KT), (0, 0), (0, 0)))
    return (grad_q, total[0].astype(jnp.bfloat16), total[1].astype(jnp.bfloat16))


def solution(mesh):
    return jax.shard_map(
        shards,
        mesh=mesh,
        in_specs=(
            P("tok", "head", None),
            P("tok", "head", None),
            P("tok", "head", None),
            P("tok", "head"),
            P("head", None),
            P("tok", None),
        ),
        out_specs=(P("tok", "head", None), P("tok", "head", None), P("tok", "head", None)),
        check_vma=False,
    )
```

profile of v0, /device:TPU:0, one launch (start us, length us, event | category | flops | bytes accessed | tf_op | source)
XLA Modules:
  0.0 246.9 jit_solution(6776335779000956911)
XLA Ops:
  7.2 0.7 compare_bitcast_fusion.1
  9.4 1.2 compare_and_fusion.1
  11.2 0.7 sub.35
  11.9 7.3 %all-to-all-start = ((s32[8,1,8]{2,1,0:T(1,128)}), s32[8,1,8]{2,1,0:T(1,128)S(1)}, u32[]{:S(2)}, u32[]{:S(2)}) async-start(s32[8,1,8]{2,1,0:T(1,128)} %bitcast.5), calls=%async_computation | async-start | bytes 8192 | tf_op jit(solution)/shard_map/all_to_all | solution.py:62
  19.2 1.2 pad_maximum_fusion.1
  20.5 5.1 %all-to-all-done = s32[8,1,8]{2,1,0:T(1,128)S(1)} async-done(((s32[8,1,8]{2,1,0:T(1,128)}), s32[8,1,8]{2,1,0:T(1,128)S(1)}, u32[]{:S(2)}, u32[]{:S(2)}) %all-to-all-start) | async-done | bytes 288 | tf_op jit(solution)/shard_map/all_to_all | solution.py:62
  25.7 2.6 %gather_fusion = bf16[64,2,16,6,128]{4,2,3,1,0:T(8,128)(2,1)} fusion(bf16[2,16,16,6,128]{4,2,3,1,0:T(8,128)(2,1)S(1)} %copy.98, s32[1024]{0:T(1024)S(1)} %pad_clamp_fusion.1), kind=kCustom, calls=%fused_computation | custom fusion | bytes 6291712 | tf_op jit(solution)/shard_map/jit(_take)/gather | solution.py:67
  28.3 2.4 copy.84
  31.2 2.2 copy.85
  33.4 3.6 %all-to-all-start.1 = ((bf16[2,8,8,16,6,128]{5,3,4,2,0,1:T(8,128)(2,1)}), bf16[2,8,8,16,6,128]{5,3,4,2,0,1:T(8,128)(2,1)S(1)}, u32[]{:S(2)}, u32[]{:S(2)}) async-start(bf16[2,8,8,16,6,128]{5,3,4,2,0,1:T(8,128)(2,1)} %copy.85), calls=%async_computation.1 | async-start | bytes 6291456 | tf_op jit(solution)/shard_map/all_to_all | solution.py:69
  37.1 0.7 all-gather.2.cloned.1.call-update
  37.8 1.4 pad_maximum_fusion.3
  39.2 4.4 %collective-permute-start = (bf16[2,16,6,128]{3,1,2,0:T(8,128)(2,1)}, bf16[2,16,6,128]{3,1,2,0:T(8,128)(2,1)}, u32[]{:S(2)}, u32[]{:S(2)}) collective-permute-start(bf16[2,16,6,128]{3,1,2,0:T(8,128)(2,1)} %get-tuple-element.32), channel_id=1, source_target_pairs={{0,4},{4,8},{8,12},{12,16},{16,20},{20,24},{24,28},{1,5},{5,9},{9,... | collective-permute-start | bytes 147464 | tf_op jit(solution)/shard_map/ppermute | solution.py:17
  43.6 1.3 collective-permute-start.1
  44.9 0.7 broadcast_in_dim.92
  45.6 0.7 broadcast_in_dim.93
  47.1 0.7 fusion.57
  47.8 1.3 fusion.66
  49.1 11.3 %all-gather.2.cloned.1.call-done = bf16[256,3072]{1,0:T(8,128)(2,1)} async-done(((bf16[256,768]{1,0:T(8,128)(2,1)}), bf16[256,3072]{1,0:T(8,128)(2,1)}) %all-gather.2.cloned.1.call-update) | async-done | bytes 1572880 | tf_op jit(solution)/shard_map/all_gather | solution.py:43
  60.5 5.0 %convolution_convert_fusion.1 = bf16[256,768]{1,0:T(8,128)(2,1)} fusion(bf16[256,3072]{1,0:T(8,128)(2,1)} %all-gather.2.cloned.1.call-done, bf16[768,3072]{1,0:T(8,128)(2,1)} %param.10), kind=kOutput, calls=%fused_computation.41 | convolution fusion | flops 1208156160 | bytes 6684672 | tf_op jit(solution)/shard_map/dot_general | solution.py:42
  65.5 1.9 copy.88
  67.4 39.7 %all-to-all-done.1 = bf16[2,8,8,16,6,128]{5,3,4,2,0,1:T(8,128)(2,1)S(1)} async-done(((bf16[2,8,8,16,6,128]{5,3,4,2,0,1:T(8,128)(2,1)}), bf16[2,8,8,16,6,128]{5,3,4,2,0,1:T(8,128)(2,1)S(1)}, u32[]{:S(2)}, u32[]{:S(2)}) %all-to-all-start.1) | async-done | bytes 3145760 | tf_op jit(solution)/shard_map/all_to_all | solution.py:69
  107.0 2.3 copy.86
  109.3 2.8 %gather_fusion.1 = bf16[40,2,16,6,128]{4,2,3,1,0:T(8,128)(2,1)S(1)} fusion(bf16[2,64,16,6,128]{4,2,3,1,0:T(8,128)(2,1)} %bitcast.130, s32[1024]{0:T(1024)S(1)} %pad_clamp_fusion), kind=kCustom, calls=%fused_computation.1 | custom fusion | bytes 3932320 | tf_op jit(solution)/shard_map/jit(_take)/gather | solution.py:77
  113.3 1.1 pad_maximum_fusion
  114.3 3.4 %fusion.34 = f32[6,256,928]{1,2,0:T(8,128)} fusion(bf16[256,6,128]{0,2,1:T(8,128)(2,1)S(1)} %bitcast.137, bf16[2,928,6,128]{3,1,2,0:T(8,128)(2,1)S(1)} %pad_maximum_fusion), kind=kOutput, calls=%fused_computation.38 | convolution fusion | flops 364904448 | bytes 7520256 | tf_op jit(solution)/shard_map/qhd,khd->hqk/dot_general | solution.py:99
  117.8 0.9 fusion.35
  118.7 1.9 fusion.69
  120.6 2.4 copy-done.12
  123.0 0.9 fusion.25
  123.9 10.8 %fusion.28 = f32[1,928,6,128]{3,1,2,0:T(8,128)} fusion(bf16[256,6,128]{2,0,1:T(8,128)(2,1)S(1)} %copy-done, f32[6,256,928]{1,2,0:T(8,128)} %fusion.34, f32[6,256,928]{1,2,0:T(8,128)} %copy-done.12, f32[6,256]{1,0:T(8,128)S(1)} %get-tuple-element.39), kind=kOutput, calls=%fused_computation.32 | convolution fusion | flops 374884768 | bytes 14653440 | tf_op jit(solution)/shard_map/hqk,qhd->khd/dot_general | solution.py:105
  134.7 4.3 %fusion.67 = (bf16[2,928,6,128]{3,1,2,0:T(8,128)(2,1)}, f32[2,928,6,128]{3,1,2,0:T(8,128)S(1)}) fusion(f32[928]{0:T(1024)S(1)} %get-tuple-element.34, f32[1,928,6,128]{3,1,2,0:T(8,128)S(1)} %fusion.25, f32[1,928,6,128]{3,1,2,0:T(8,128)} %fusion.28), kind=kLoop, calls=%fused_computation.110 | loop fusion | flops 4276224 | bytes 14257792 | tf_op jit(solution)/shard_map/convert.7
  139.3 2.2 copy-done.2
  141.5 4.7 %copy.91 = f32[2,640,6,128]{3,2,1,0:T(8,128)} copy(f32[2,640,6,128]{3,1,2,0:T(8,128)S(1)} %slice.51) | data formatting | bytes 7864320 | tf_op jit(solution)/shard_map/slice | solution.py:111
  146.2 5.7 %reshape.296 = f32[2,40,12288]{2,1,0:T(8,128)} reshape(f32[2,640,6,128]{3,2,1,0:T(8,128)} %copy.91) | data formatting | bytes 7864320 | tf_op jit(solution)/shard_map/reshape | solution.py:111
  151.9 5.0 %fusion.2 = bf16[2,8,8,12288]{3,2,1,0:T(8,128)(2,1)S(1)} fusion(f32[2,40,12288]{2,1,0:T(8,128)} %reshape.296, s32[40]{0:T(128)S(1)} %copy-done.8, pred[40]{0:T(512)(128)(4,1)S(1)} %get-tuple-element.36), kind=kOutput, calls=%fused_computation.5 | convolution fusion | flops 756552704 | bytes 7078088 | tf_op jit(solution)/shard_map/cs,ecr->esr/dot_general | solution.py:112
  156.9 1.9 copy.92
  158.8 3.8 %all-to-all-start.2 = ((bf16[2,8,8,12288]{3,2,0,1:T(8,128)(2,1)}), bf16[2,8,8,12288]{3,2,0,1:T(8,128)(2,1)S(1)}, u32[]{:S(2)}, u32[]{:S(2)}) async-start(bf16[2,8,8,12288]{3,2,0,1:T(8,128)(2,1)} %copy.92), calls=%async_computation.2 | async-start | bytes 6291456 | tf_op jit(solution)/shard_map/all_to_all | solution.py:115
  163.8 10.0 %fusion.39 = bf16[256,6,128]{0,2,1:T(8,128)(2,1)S(1)} fusion(f32[6,256,928]{1,2,0:T(8,128)} %fusion.34, bf16[2,928,6,128]{3,1,2,0:T(8,128)(2,1)} %copy-done.3, f32[6,256,928]{1,2,0:T(8,128)} %copy-done.12, f32[6,256]{1,0:T(8,128)S(1)} %copy-done.14), kind=kOutput, calls=%fused_computation.43 | convolution fusion | flops 375081376 | bytes 24641536 | tf_op jit(solution)/shard_map/hqk,khd->qhd/dot_general | solution.py:102
  173.8 0.9 copy.95
  174.7 1.5 fusion.68
  176.2 1.3 collective-permute-start.2
  177.5 5.2 %collective-permute-start.3 = (bf16[2,16,6,128]{3,1,2,0:T(8,128)(2,1)}, bf16[2,16,6,128]{3,1,2,0:T(8,128)(2,1)}, u32[]{:S(2)}, u32[]{:S(2)}) collective-permute-start(bf16[2,16,6,128]{3,1,2,0:T(8,128)(2,1)} %get-tuple-element.29), channel_id=1, source_target_pairs={{0,4},{4,8},{8,12},{12,16},{16,20},{20,24},{24,28},{1,5},{5,9},{9,... | collective-permute-start | bytes 147464 | tf_op jit(solution)/shard_map/ppermute | solution.py:29
  182.6 50.8 %all-to-all-done.2 = bf16[2,8,8,12288]{3,2,0,1:T(8,128)(2,1)S(1)} async-done(((bf16[2,8,8,12288]{3,2,0,1:T(8,128)(2,1)}), bf16[2,8,8,12288]{3,2,0,1:T(8,128)(2,1)S(1)}, u32[]{:S(2)}, u32[]{:S(2)}) %all-to-all-start.2) | async-done | bytes 3145760 | tf_op jit(solution)/shard_map/all_to_all | solution.py:115
  233.4 1.7 convolution_bitcast_fusion
  235.1 2.2 reshape.299
  237.3 1.8 fusion.33
  239.1 0.9 slice_bitcast_fusion.9
  (58 shorter events, 6.3 us)
Async XLA Ops:
  7.2 110.6 %copy-start = (bf16[256,6,128]{2,0,1:T(8,128)(2,1)S(1)}, bf16[256,6,128]{2,0,1:T(8,128)(2,1)}, u32[]{:S(2)}) copy-start(bf16[256,6,128]{2,0,1:T(8,128)(2,1)} %param.6) | copy-start | bytes 1179652
  9.4 1.8 copy-start.10
  10.6 0.5 copy-start.7
  11.9 13.7 %all-to-all-start = ((s32[8,1,8]{2,1,0:T(1,128)}), s32[8,1,8]{2,1,0:T(1,128)S(1)}, u32[]{:S(2)}, u32[]{:S(2)}) async-start(s32[8,1,8]{2,1,0:T(1,128)} %bitcast.5), calls=%async_computation | async-start | bytes 8192 | tf_op jit(solution)/shard_map/all_to_all | solution.py:62
  33.4 73.7 %all-to-all-start.1 = ((bf16[2,8,8,16,6,128]{5,3,4,2,0,1:T(8,128)(2,1)}), bf16[2,8,8,16,6,128]{5,3,4,2,0,1:T(8,128)(2,1)S(1)}, u32[]{:S(2)}, u32[]{:S(2)}) async-start(bf16[2,8,8,16,6,128]{5,3,4,2,0,1:T(8,128)(2,1)} %copy.85), calls=%async_computation.1 | async-start | bytes 6291456 | tf_op jit(solution)/shard_map/all_to_all | solution.py:69
  37.0 23.4 %all-gather.2.cloned.1.call-start = ((), (), s32[]{:S(2)}) async-start(), calls=%async_computation.3 | async-start | bytes 1966080 | tf_op jit(solution)/shard_map/all_gather | solution.py:43
  39.2 73.9 %collective-permute-start = (bf16[2,16,6,128]{3,1,2,0:T(8,128)(2,1)}, bf16[2,16,6,128]{3,1,2,0:T(8,128)(2,1)}, u32[]{:S(2)}, u32[]{:S(2)}) collective-permute-start(bf16[2,16,6,128]{3,1,2,0:T(8,128)(2,1)} %get-tuple-element.32), channel_id=1, source_target_pairs={{0,4},{4,8},{8,12},{12,16},{16,20},{20,24},{24,28},{1,5},{5,9},{9,... | collective-permute-start | bytes 147464 | tf_op jit(solution)/shard_map/ppermute | solution.py:17
  43.6 69.5 %collective-permute-start.1 = (bf16[2,16,6,128]{3,1,2,0:T(8,128)(2,1)}, bf16[2,16,6,128]{3,1,2,0:T(8,128)(2,1)}, u32[]{:S(2)}, u32[]{:S(2)}) collective-permute-start(bf16[2,16,6,128]{3,1,2,0:T(8,128)(2,1)} %get-tuple-element.33), channel_id=1, source_target_pairs={{4,0},{8,4},{12,8},{16,12},{20,16},{24,20},{28,24},{5,1},{9,5},{13... | collective-permute-start | bytes 147464 | tf_op jit(solution)/shard_map/ppermute | solution.py:19
  109.3 3.3 %copy-start.9 = (pred[640]{0:T(1024)(128)(4,1)S(1)}, pred[640]{0:T(1024)(128)(4,1)}, u32[]{:S(2)}) copy-start(pred[640]{0:T(1024)(128)(4,1)} %broadcast_in_dim.93) | copy-start | bytes 1924
  112.1 1.0 copy-start.4
  112.1 1.1 copy-start.5
  112.6 1.7 copy-start.6
  114.3 4.4 %copy-start.3 = (bf16[2,928,6,128]{3,1,2,0:T(8,128)(2,1)}, bf16[2,928,6,128]{3,1,2,0:T(8,128)(2,1)S(1)}, u32[]{:S(2)}) copy-start(bf16[2,928,6,128]{3,1,2,0:T(8,128)(2,1)S(1)} %pad_maximum_fusion) | copy-start | bytes 8552452
  117.8 0.9 copy-start.11
  120.6 2.4 copy-start.12
  120.6 3.3 %copy-start.13 = (f32[6,256]{1,0:T(8,128)}, f32[6,256]{1,0:T(8,128)S(1)}, u32[]{:S(2)}) copy-start(f32[6,256]{1,0:T(8,128)S(1)} %get-tuple-element.39) | copy-start | bytes 18436
  139.1 2.5 copy-start.2
  146.2 5.7 %copy-start.8 = (s32[40]{0:T(128)S(1)}, s32[40]{0:T(128)}, u32[]{:S(2)}) copy-start(s32[40]{0:T(128)} %copy-done.7) | copy-start | bytes 484
  158.8 5.1 %copy-start.14 = (f32[6,256]{1,0:T(8,128)S(1)}, f32[6,256]{1,0:T(8,128)}, u32[]{:S(2)}) copy-start(f32[6,256]{1,0:T(8,128)} %copy-done.13) | copy-start | bytes 18436
  158.8 74.6 %all-to-all-start.2 = ((bf16[2,8,8,12288]{3,2,0,1:T(8,128)(2,1)}), bf16[2,8,8,12288]{3,2,0,1:T(8,128)(2,1)S(1)}, u32[]{:S(2)}, u32[]{:S(2)}) async-start(bf16[2,8,8,12288]{3,2,0,1:T(8,128)(2,1)} %copy.92), calls=%async_computation.2 | async-start | bytes 6291456 | tf_op jit(solution)/shard_map/all_to_all | solution.py:115
  176.2 61.1 %collective-permute-start.2 = (bf16[2,16,6,128]{3,1,2,0:T(8,128)(2,1)}, bf16[2,16,6,128]{3,1,2,0:T(8,128)(2,1)}, u32[]{:S(2)}, u32[]{:S(2)}) collective-permute-start(bf16[2,16,6,128]{3,1,2,0:T(8,128)(2,1)} %get-tuple-element.28), channel_id=1, source_target_pairs={{4,0},{8,4},{12,8},{16,12},{20,16},{24,20},{28,24},{5,1},{9,5},{13... | collective-permute-start | bytes 147464 | tf_op jit(solution)/shard_map/ppermute | solution.py:29
  177.5 59.8 %collective-permute-start.3 = (bf16[2,16,6,128]{3,1,2,0:T(8,128)(2,1)}, bf16[2,16,6,128]{3,1,2,0:T(8,128)(2,1)}, u32[]{:S(2)}, u32[]{:S(2)}) collective-permute-start(bf16[2,16,6,128]{3,1,2,0:T(8,128)(2,1)} %get-tuple-element.29), channel_id=1, source_target_pairs={{0,4},{4,8},{8,12},{12,16},{16,20},{20,24},{24,28},{1,5},{5,9},{9,... | collective-permute-start | bytes 147464 | tf_op jit(solution)/shard_map/ppermute | solution.py:29
  235.1 4.9 %copy-start.1 = (bf16[256,6,128]{2,0,1:T(8,128)(2,1)S(1)}, bf16[256,6,128]{2,0,1:T(8,128)(2,1)}, u32[]{:S(2)}) copy-start(bf16[256,6,128]{2,0,1:T(8,128)(2,1)} %param.6) | copy-start | bytes 1179652
Sparse Core Ops, SparseCore 0:
  39.4 20.9 all-gather.1
where the time goes:
time: 248 us; the launch traced here: 247 us
  waiting for transfers between devices  108 us (44%)
  local copies, waits for them, and re-layouts  41.7 us (17%)
  matrix products  37.7 us (15%)
  starting transfers between devices  26.9 us (11%)
  other arithmetic  18.8 us (8%)
  between operations  14.4 us (6%)
    all_to_all x1, waiting for transfers between devices, shards(): lax.all_to_all(slotted.reshape(2, count, capacity, row_len).astype(jnp.bf...  50.8 us
    all_to_all x1, waiting for transfers between devices, shards(): lax.all_to_all(served.reshape(2, count, capacity, KT, heads_here, head_di...  39.7 us
    all_gather x1, waiting for transfers between devices, shards(): lax.all_gather(grad_out, 'head', axis=1, tiled=True)  11.3 us
    dot_general x1, matrix products, shards(): jnp.einsum('hqk,qhd->khd', dscore, queries, preferred_element_type=jnp.fl...  10.8 us
    dot_general x1, matrix products, shards(): jnp.einsum('hqk,khd->qhd', dscore, key_all, preferred_element_type=jnp.fl...  9.97 us
    all_to_all x1, starting transfers between devices, shards(): lax.all_to_all(request.reshape(count, capacity), 'tok', split_axis=0, con...  7.28 us
    ppermute x2, starting transfers between devices, shifted(): lax.ppermute(value, axis, [(source, source + steps) for source in range(l...  6.44 us
    unnamed x31, local copies, waits for them, and re-layouts  6.22 us
  transfers between devices with their start and end apart: 8, of which 4 were waited for; matrix products, arithmetic and copies ran while one was open for 15% of the time, Pallas kernels for 0%

commit v1 on v0

--- a/solution.py
+++ b/solution.py
@@ -1,9 +1,365 @@
+import functools
+
 import jax
 import jax.numpy as jnp
 from jax import lax
+from jax.experimental import pallas as pl
+from jax.experimental.pallas import tpu as pltpu
 from jax.sharding import PartitionSpec as P
 
 KT = 16
+LANES = 128
+MASKED = -1e30
+MESH = pl.DeviceIdType.MESH
+NT = (((1,), (1,)), ((), ()))
+
+
+def owner_of(h, group, count, heads):
+    gap = count - heads
+    odd = group % 2
+    late = jnp.where(h >= heads // 2, gap, 0)
+    return h + jnp.where(odd == 1, late, gap // 2)
+
+
+def head_of(me, group, count, heads):
+    gap = count - heads
+    half = heads // 2
+    odd = group % 2
+    even_head = me - gap // 2
+    odd_head = jnp.where(me < half, me, me - gap)
+    even_owns = (even_head >= 0) & (even_head < heads)
+    odd_owns = (me < half) | (me >= half + gap)
+    owns = ((odd == 1) & odd_owns) | ((odd == 0) & even_owns)
+    head = jnp.where(odd == 1, odd_head, even_head)
+    return jnp.clip(head, 0, heads - 1), owns
+
+
+def by_head_kernel(
+    count, groups, ncrit, crit, q_in, k_in, v_in, go_in, w_in, dq_out, dk_out, dv_out,
+    q_all, k_all, v_all, d_all, bias_own, bias_all, go_all, w_all, acc, d_own, onehot, k_turned,
+    weights, scores, dprob, inverse, dk_acc, dv_acc, dq_st, dk_st, dv_st,
+    send_in, recv_in, send_go, recv_go, w_sem, send_out, recv_out,
+):
+    heads, rows, dim = q_in.shape
+    total = count * rows
+    tiles_here = rows // KT
+    width = go_in.shape[1]
+    me = lax.axis_index("tok")
+    group = lax.axis_index("head")
+    head, owns = head_of(me, group, count, heads)
+
+    barrier = pltpu.get_barrier_semaphore()
+    for step in range(1, count):
+        pl.semaphore_signal(
+            barrier, inc=1, device_id=((me + step) % count, group), device_id_type=MESH
+        )
+    for step in range(1, groups):
+        pl.semaphore_signal(
+            barrier, inc=1, device_id=(me, (group + step) % groups), device_id_type=MESH
+        )
+    loads = []
+    for s in range(groups):
+        load = pltpu.make_async_copy(w_in.at[:, pl.ds(s * width, width)], w_all.at[s], w_sem.at[s])
+        load.start()
+        loads.append(load)
+    tile_ids = lax.broadcasted_iota(jnp.int32, (KT, LANES), 1)
+    first = me * tiles_here - 1
+    allowed = (tile_ids >= first) & (tile_ids <= first + tiles_here + 1)
+    for c in range(ncrit):
+        allowed = allowed | (tile_ids == crit[0, c])
+    bias_own[...] = jnp.where(allowed, 0.0, MASKED).astype(jnp.bfloat16)
+    pl.semaphore_wait(barrier, count - 1 + groups - 1)
+
+    def go_copy(step):
+        return pltpu.make_async_remote_copy(
+            src_ref=go_in,
+            dst_ref=go_all.at[group],
+            send_sem=send_go.at[step],
+            recv_sem=recv_go.at[step],
+            device_id=(me, (group + step) % groups),
+            device_id_type=MESH,
+        )
+
+    for step in range(1, groups):
+        go_copy(step).start()
+    own_go = pltpu.make_async_copy(go_in, go_all.at[group], recv_go.at[0])
+    own_go.start()
+
+    here = pl.ds(pl.multiple_of(me * rows, rows), rows)
+
+    def target(i):
+        half = heads // 2
+        far = jnp.where(me < count // 2, half, 0)
+        h = (far + (i % half + me) % half + (i // half) * half) % heads
+        return h, owner_of(h, group, count, heads)
+
+    def in_copy(kind, src, dst, h, owner):
+        return pltpu.make_async_remote_copy(
+            src_ref=src,
+            dst_ref=dst,
+            send_sem=send_in.at[kind, h],
+            recv_sem=recv_in.at[kind, me],
+            device_id=(owner, group),
+            device_id_type=MESH,
+        )
+
+    def send(kind, src, dst, h, owner):
+        @pl.when(owner != me)
+        def _():
+            in_copy(kind, src, dst, h, owner).start()
+
+        @pl.when(owner == me)
+        def _():
+            pltpu.make_async_copy(src, dst, recv_in.at[kind, me]).start()
+
+    for i in range(heads):
+        h, owner = target(i)
+        send(4, bias_own, bias_all.at[me], h, owner)
+        send(0, k_in.at[h], k_all.at[here], h, owner)
+    for i in range(heads):
+        h, owner = target(i)
+        send(1, q_in.at[h], q_all.at[here], h, owner)
+    for i in range(heads):
+        h, owner = target(i)
+        send(2, v_in.at[h], v_all.at[here], h, owner)
+
+    for step in range(groups):
+        src = (group + groups - step) % groups
+        if step == 0:
+            own_go.wait()
+        else:
+            go_copy(step).wait_recv()
+        if step == 0:
+            for load in loads:
+                load.wait()
+        part = lax.dot_general(
+            go_all[src], w_all[src], NT, preferred_element_type=jnp.float32
+        )
+        if step == 0:
+            acc[...] = part
+        elif step < groups - 1:
+            acc[...] += part
+        else:
+            done = (acc[...] + part).astype(jnp.bfloat16)
+            for h in range(heads):
+                d_own[h] = done[:, h * dim : (h + 1) * dim]
+    for i in range(heads):
+        h, owner = target(i)
+        send(3, d_own.at[h], d_all.at[here], h, owner)
+
+    def landed(kind, dst, b):
+        in_copy_from = pltpu.make_async_remote_copy(
+            src_ref=dst,
+            dst_ref=dst,
+            send_sem=send_in.at[kind, 0],
+            recv_sem=recv_in.at[kind, b],
+            device_id=((me + 1) % count, group),
+            device_id_type=MESH,
+        )
+        in_copy_from.wait_recv()
+
+    def block(b):
+        return pl.ds(pl.multiple_of(b * rows, rows), rows)
+
+    scale = dim ** (-0.5)
+
+    @pl.when(owns)
+    def _():
+        def prepare(b, carry):
+            landed(4, bias_all.at[b], b)
+            landed(0, k_all.at[block(b)], b)
+            ids = lax.broadcasted_iota(jnp.int32, (rows, LANES), 1)
+            of_row = b * tiles_here + lax.broadcasted_iota(jnp.int32, (rows, LANES), 0) // KT
+            onehot[block(b), :] = jnp.where(ids == of_row, 1.0, 0.0).astype(jnp.bfloat16)
+            k_turned[b] = k_all[block(b), :].T
+            return carry
+
+        lax.fori_loop(0, count, prepare, 0)
+
+        def forward(b, carry):
+            landed(1, q_all.at[block(b)], b)
+            bias = jnp.broadcast_to(bias_all[b][0:1, :], (rows, LANES))
+            query = jnp.concatenate([q_all[block(b), :], bias], axis=1)
+            top = jnp.full((8, rows), MASKED, jnp.float32)
+            for j in range(count):
+                at = slice(j * rows, (j + 1) * rows)
+                key = jnp.concatenate([k_all[at, :], onehot[at, :]], axis=1)
+                s = lax.dot_general(key, query, NT, preferred_element_type=jnp.float32)
+                scores[at, :] = s
+                top = jnp.maximum(top, jnp.max(s.reshape(rows // 8, 8, rows), axis=0))
+            top = jnp.max(top, axis=0, keepdims=True)
+            factor = scale * 1.4426950408889634
+            summed = jnp.zeros((8, rows), jnp.float32)
+            for j in range(count):
+                at = slice(j * rows, (j + 1) * rows)
+                e = jnp.exp2((scores[at, :] - top) * factor)
+                weights[b, at, :] = e.astype(jnp.bfloat16)
+                summed = summed + jnp.sum(e.reshape(rows // 8, 8, rows), axis=0)
+            inv = 1.0 / jnp.sum(summed, axis=0, keepdims=True)
+            inverse[b] = jnp.broadcast_to(inv, (8, rows))
+            return carry
+
+        lax.fori_loop(0, count, forward, 0)
+        dk_acc[...] = jnp.zeros_like(dk_acc)
+        dv_acc[...] = jnp.zeros_like(dv_acc)
+
+        def values_in(b, carry):
+            landed(2, v_all.at[block(b)], b)
+            return carry
+
+        lax.fori_loop(0, count, values_in, 0)
+
+        def backward(b, carry):
+            landed(3, d_all.at[block(b)], b)
+            d_b = d_all[block(b), :]
+            q_b = q_all[block(b), :]
+            inv = inverse[b][0:1, :]
+            delta = jnp.zeros((8, rows), jnp.float32)
+            for j in range(count):
+                at = slice(j * rows, (j + 1) * rows)
+                dp = lax.dot_general(v_all[at, :], d_b, NT, preferred_element_type=jnp.float32)
+                dprob[at, :] = dp
+                w = weights[b, at, :].astype(jnp.float32) * dp
+                delta = delta + jnp.sum(w.reshape(rows // 8, 8, rows), axis=0)
+            delta = jnp.sum(delta, axis=0, keepdims=True) * inv
+            dq = jnp.zeros((dim, rows), jnp.float32)
+            for j in range(count):
+                at = slice(j * rows, (j + 1) * rows)
+                p = weights[b, at, :].astype(jnp.float32) * inv
+                ds = (p * (dprob[at, :] - delta)).astype(jnp.bfloat16)
+                dv_acc[at, :] += jnp.dot(
+                    p.astype(jnp.bfloat16), d_b, preferred_element_type=jnp.float32
+                )
+                dk_acc[at, :] += jnp.dot(ds, q_b, preferred_element_type=jnp.float32)
+                dq = dq + jnp.dot(k_turned[j], ds, preferred_element_type=jnp.float32)
+            dq_st[block(b), :] = (dq * scale).T.astype(jnp.bfloat16)
+            give(0, dq_st, dq_out, b)
+            return carry
+
+        def out_copy(kind, staged, out, b):
+            return pltpu.make_async_remote_copy(
+                src_ref=staged.at[block(b)],
+                dst_ref=out.at[head],
+                send_sem=send_out.at[kind, b],
+                recv_sem=recv_out.at[kind, head],
+                device_id=(b, group),
+                device_id_type=MESH,
+            )
+
+        def give(kind, staged, out, b):
+            @pl.when(b != me)
+            def _():
+                out_copy(kind, staged, out, b).start()
+
+            @pl.when(b == me)
+            def _():
+                pltpu.make_async_copy(
+                    staged.at[block(b)], out.at[head], recv_out.at[kind, head]
+                ).start()
+
+        lax.fori_loop(0, count, backward, 0)
+
+        def finish(i, carry):
+            b = (me + count // 2 + i) % count
+            dk_st[block(b), :] = (dk_acc[block(b), :] * scale).astype(jnp.bfloat16)
+            give(1, dk_st, dk_out, b)
+            dv_st[block(b), :] = dv_acc[block(b), :].astype(jnp.bfloat16)
+            give(2, dv_st, dv_out, b)
+            return carry
+
+        lax.fori_loop(0, count, finish, 0)
+
+        def sent(b, carry):
+            @pl.when(b != me)
+            def _():
+                for kind, staged, out in ((0, dq_st, dq_out), (1, dk_st, dk_out), (2, dv_st, dv_out)):
+                    out_copy(kind, staged, out, b).wait_send()
+
+            return carry
+
+        lax.fori_loop(0, count, sent, 0)
+
+    for step in range(1, groups):
+        go_copy(step).wait_send()
+    for h in range(heads):
+        owner = owner_of(h, group, count, heads)
+
+        @pl.when(owner != me)
+        def _():
+            in_copy(0, k_in.at[h], k_all.at[here], h, owner).wait_send()
+            in_copy(1, q_in.at[h], q_all.at[here], h, owner).wait_send()
+            in_copy(2, v_in.at[h], v_all.at[here], h, owner).wait_send()
+            in_copy(3, d_own.at[h], d_all.at[here], h, owner).wait_send()
+            in_copy(4, bias_own, bias_all.at[me], h, owner).wait_send()
+
+        for kind, out in ((0, dq_out), (1, dk_out), (2, dv_out)):
+            pltpu.make_async_remote_copy(
+                src_ref=out.at[h],
+                dst_ref=out.at[h],
+                send_sem=send_out.at[kind, 0],
+                recv_sem=recv_out.at[kind, h],
+                device_id=((me + 1) % count, group),
+                device_id_type=MESH,
+            ).wait_recv()
+
+
+def by_head(queries, keys, values, grad_out, w_out, crit):
+    rows, heads, dim = queries.shape
+    count = lax.axis_size("tok")
+    groups = lax.axis_size("head")
+    total = count * rows
+    width = grad_out.shape[1]
+    bf16, f32 = jnp.bfloat16, jnp.float32
+    anywhere = pl.BlockSpec(memory_space=pl.ANY)
+    vmem, dma = pltpu.VMEM, pltpu.SemaphoreType.DMA
+    out = jax.ShapeDtypeStruct((heads, rows, dim), bf16)
+    grads = pl.pallas_call(
+        functools.partial(by_head_kernel, count, groups, crit.shape[1]),
+        out_shape=(out, out, out),
+        in_specs=[pl.BlockSpec(memory_space=pltpu.SMEM)] + [anywhere] * 5,
+        out_specs=(anywhere, anywhere, anywhere),
+        scratch_shapes=[
+            vmem((total, dim), bf16),
+            vmem((total, dim), bf16),
+            vmem((total, dim), bf16),
+            vmem((total, dim), bf16),
+            vmem((KT, LANES), bf16),
+            vmem((count, KT, LANES), bf16),
+            vmem((groups, rows, width), bf16),
+            vmem((groups, w_out.shape[0], width), bf16),
+            vmem((rows, heads * dim), f32),
+            vmem((heads, rows, dim), bf16),
+            vmem((total, LANES), bf16),
+            vmem((count, dim, rows), bf16),
+            vmem((count, total, rows), bf16),
+            vmem((total, rows), f32),
+            vmem((total, rows), f32),
+            vmem((count, 8, rows), f32),
+            vmem((total, dim), f32),
+            vmem((total, dim), f32),
+            vmem((total, dim), bf16),
+            vmem((total, dim), bf16),
+            vmem((total, dim), bf16),
+            dma((5, heads)),
+            dma((5, count)),
+            dma((groups,)),
+            dma((groups,)),
+            dma((groups,)),
+            dma((3, count)),
+            dma((3, heads)),
+        ],
+        compiler_params=pltpu.CompilerParams(
+            collective_id=0, has_side_effects=True, vmem_limit_bytes=52 * 2**20
+        ),
+    )(
+        crit,
+        jnp.transpose(queries, (1, 0, 2)),
+        jnp.transpose(keys, (1, 0, 2)),
+        jnp.transpose(values, (1, 0, 2)),
+        grad_out,
+        w_out,
+    )
+    return tuple(jnp.transpose(grad, (1, 0, 2)) for grad in grads)
 
 
 def padded(cells, sides, width):
@@ -35,6 +391,8 @@
     count = lax.axis_size("tok")
     place = lax.axis_index("tok")
     tiles_here = tok_rows // KT
+    if heads_here <= count <= 2 * heads_here and count * tiles_here <= LANES:
+        return by_head(queries, keys, values, grad_out, w_out, crit)
     ncrit = crit.shape[1]
     capacity = (ncrit + count - 4) // (count - 3)
     slots = count * capacity

time: 248 us -> 77.4 us (0.31)
  the two profiles are of different devices: /device:TPU:0 before, /device:TPU:24 now
where the time goes in v1:
time: 77.4 us; the launch traced here: 77.1 us
  Pallas kernels  71.6 us (93%)
  local copies, waits for them, and re-layouts  4.88 us (6%)
    pallas_call x1, Pallas kernels, by_head(): pl.pallas_call(functools.partial(by_head_kernel, count, groups, crit.shap...  71.6 us
    unnamed x9, local copies, waits for them, and re-layouts  4.88 us

profile of v1, /device:TPU:24, one launch (start us, length us, event | category | flops | bytes accessed | tf_op | source)
XLA Modules:
  0.0 77.1 jit_solution(15151956813303292301)
XLA Ops:
  0.6 0.0 copy-start
  0.6 1.0 %copy-done = bf16[256,6,128]{2,0,1:T(8,128)(2,1)S(1)} copy-done((bf16[256,6,128]{2,0,1:T(8,128)(2,1)S(1)}, bf16[256,6,128]{2,0,1:T(8,128)(2,1)}, u32[]{:S(2)}) %copy-start) | copy-done | bytes 393240
  1.6 0.0 copy-start.1
  1.6 1.0 %copy-done.1 = bf16[256,6,128]{2,0,1:T(8,128)(2,1)S(1)} copy-done((bf16[256,6,128]{2,0,1:T(8,128)(2,1)S(1)}, bf16[256,6,128]{2,0,1:T(8,128)(2,1)}, u32[]{:S(2)}) %copy-start.1) | copy-done | bytes 393240
  2.6 0.0 copy-start.2
  2.6 0.7 copy-done.2
  3.3 71.6 %shard_map.85 = (bf16[6,256,128]{2,1,0:T(8,128)(2,1)S(1)}, bf16[6,256,128]{2,1,0:T(8,128)(2,1)S(1)}, bf16[6,256,128]{2,1,0:T(8,128)(2,1)S(1)}) custom-call(s32[1,40]{1,0:T(1,128)S(1)} %copy-done.2, bf16[6,256,128]{2,1,0:T(8,128)(2,1)S(1)} %bitcast.6, bf16[6,256,128]{2,1,0:T(8,128)(2,1)S(1)} %bitcast.7, bf16[6,256,128]{2,1,0:T(8,128)(2,1)} %bitcast.11, ...), custom_call_target="tpu_custom_call" | custom-call | tf_op jit(solution)/shard_map/pallas_call | solution.py:316
  74.9 0.7 copy.12
  75.6 0.7 copy.13
  76.4 0.7 copy.14
Async XLA Ops:
  0.6 1.0 %copy-start = (bf16[256,6,128]{2,0,1:T(8,128)(2,1)S(1)}, bf16[256,6,128]{2,0,1:T(8,128)(2,1)}, u32[]{:S(2)}) copy-start(bf16[256,6,128]{2,0,1:T(8,128)(2,1)} %param.6) | copy-start | bytes 1179652
  1.6 1.0 %copy-start.1 = (bf16[256,6,128]{2,0,1:T(8,128)(2,1)S(1)}, bf16[256,6,128]{2,0,1:T(8,128)(2,1)}, u32[]{:S(2)}) copy-start(bf16[256,6,128]{2,0,1:T(8,128)(2,1)} %param.7) | copy-start | bytes 1179652
  2.6 0.7 copy-start.2

commit v2 on v1

--- a/solution.py
+++ b/solution.py
@@ -35,13 +35,12 @@
 
 
 def by_head_kernel(
-    count, groups, ncrit, crit, q_in, k_in, v_in, go_in, w_in, dq_out, dk_out, dv_out,
-    q_all, k_all, v_all, d_all, bias_own, bias_all, go_all, w_all, acc, d_own, onehot, k_turned,
-    weights, scores, dprob, inverse, dk_acc, dv_acc, dq_st, dk_st, dv_st,
-    send_in, recv_in, send_go, recv_go, w_sem, send_out, recv_out,
+    count, groups, ncrit, crit, q_in, k_in, v_in, go_in, w_in, grads,
+    q_all, k_all, v_all, d_all, info_own, info_all, info, go_all, w_all, acc, d_own, onehot, k_sel,
+    k_turned, v_sel, weights, scores, dprob, inverse, dk_part, dv_part, dq_st, dk_st, dv_st,
+    info_sem, send_in, recv_in, send_go, recv_go, w_sem, send_out, recv_out,
 ):
     heads, rows, dim = q_in.shape
-    total = count * rows
     tiles_here = rows // KT
     width = go_in.shape[1]
     me = lax.axis_index("tok")
@@ -53,39 +52,49 @@
         pl.semaphore_signal(
             barrier, inc=1, device_id=((me + step) % count, group), device_id_type=MESH
         )
-    for step in range(1, groups):
-        pl.semaphore_signal(
-            barrier, inc=1, device_id=(me, (group + step) % groups), device_id_type=MESH
-        )
+    mate = group + 1 - 2 * (group % 2)
+    across = (group + groups // 2) % groups
+    for other in (mate, across):
+        pl.semaphore_signal(barrier, inc=1, device_id=(me, other), device_id_type=MESH)
     loads = []
     for s in range(groups):
         load = pltpu.make_async_copy(w_in.at[:, pl.ds(s * width, width)], w_all.at[s], w_sem.at[s])
         load.start()
         loads.append(load)
-    tile_ids = lax.broadcasted_iota(jnp.int32, (KT, LANES), 1)
+    near = tiles_here + 2
+    slots = weights.shape[1] // KT
+    chunks = weights.shape[1] // rows
+    lane = lax.broadcasted_iota(jnp.int32, (8, LANES), 1)
     first = me * tiles_here - 1
-    allowed = (tile_ids >= first) & (tile_ids <= first + tiles_here + 1)
+    tile_in = first + lane
+    tile_in = jnp.where((lane < near) & (tile_in >= 0) & (tile_in < count * tiles_here), tile_in, -1)
+    slot_of = jnp.where((lane >= first) & (lane < first + near), lane - first, slots - 1)
     for c in range(ncrit):
-        allowed = allowed | (tile_ids == crit[0, c])
-    bias_own[...] = jnp.where(allowed, 0.0, MASKED).astype(jnp.bfloat16)
-    pl.semaphore_wait(barrier, count - 1 + groups - 1)
+        tile_in = jnp.where(lane == near + c, crit[0, c], tile_in)
+        slot_of = jnp.where(lane == crit[0, c], near + c, slot_of)
+    row = lax.broadcasted_iota(jnp.int32, (8, LANES), 0)
+    info_own[...] = jnp.where(row == 0, jnp.maximum(tile_in, 0), jnp.where(row == 1, slot_of, tile_in))
+    pl.semaphore_wait(barrier, count - 1 + 2)
 
     def go_copy(step):
+        to = across if step == 2 else mate
+        shard = across if step == 3 else group
         return pltpu.make_async_remote_copy(
-            src_ref=go_in,
-            dst_ref=go_all.at[group],
+            src_ref=go_all.at[across] if step == 3 else go_in,
+            dst_ref=go_all.at[shard],
             send_sem=send_go.at[step],
             recv_sem=recv_go.at[step],
-            device_id=(me, (group + step) % groups),
+            device_id=(me, to),
             device_id_type=MESH,
         )
 
-    for step in range(1, groups):
-        go_copy(step).start()
+    go_copy(2).start()
+    go_copy(1).start()
     own_go = pltpu.make_async_copy(go_in, go_all.at[group], recv_go.at[0])
     own_go.start()
 
     here = pl.ds(pl.multiple_of(me * rows, rows), rows)
+    own_tiles = pl.ds(me * tiles_here, tiles_here)
 
     def target(i):
         half = heads // 2
@@ -114,21 +123,23 @@
 
     for i in range(heads):
         h, owner = target(i)
-        send(4, bias_own, bias_all.at[me], h, owner)
-        send(0, k_in.at[h], k_all.at[here], h, owner)
+        send(4, info_own, info_all.at[me], h, owner)
+        send(0, k_in.at[h], k_all.at[own_tiles], h, owner)
     for i in range(heads):
         h, owner = target(i)
         send(1, q_in.at[h], q_all.at[here], h, owner)
     for i in range(heads):
         h, owner = target(i)
-        send(2, v_in.at[h], v_all.at[here], h, owner)
+        send(2, v_in.at[h], v_all.at[own_tiles], h, owner)
 
     for step in range(groups):
-        src = (group + groups - step) % groups
+        src = (group, mate, across, (mate + groups // 2) % groups)[step]
         if step == 0:
             own_go.wait()
         else:
             go_copy(step).wait_recv()
+        if step == 2:
+            go_copy(3).start()
         if step == 0:
             for load in loads:
                 load.wait()
@@ -161,36 +172,63 @@
     def block(b):
         return pl.ds(pl.multiple_of(b * rows, rows), rows)
 
+    def tiles_of(b):
+        return pl.ds(b * tiles_here, tiles_here)
+
     scale = dim ** (-0.5)
+    low = me < count // 2
+
+    def near_first(i):
+        return jnp.where(low, i, count - 1 - i)
 
     @pl.when(owns)
     def _():
+        def arrived(b, carry):
+            landed(4, info_all.at[b], b)
+            landed(0, k_all.at[tiles_of(b)], b)
+            return carry
+
+        lax.fori_loop(0, count, arrived, 0)
+        to_scalars = pltpu.make_async_copy(info_all, info, info_sem)
+        to_scalars.start()
+        to_scalars.wait()
+
+        def pick(source, chosen, b):
+            for s in range(slots):
+                chosen[b, s * KT : (s + 1) * KT, :] = source[info[b, 0, s]]
+
         def prepare(b, carry):
-            landed(4, bias_all.at[b], b)
-            landed(0, k_all.at[block(b)], b)
-            ids = lax.broadcasted_iota(jnp.int32, (rows, LANES), 1)
-            of_row = b * tiles_here + lax.broadcasted_iota(jnp.int32, (rows, LANES), 0) // KT
-            onehot[block(b), :] = jnp.where(ids == of_row, 1.0, 0.0).astype(jnp.bfloat16)
-            k_turned[b] = k_all[block(b), :].T
+            pick(k_all, k_sel, b)
+            for j in range(chunks):
+                at = slice(j * rows, (j + 1) * rows)
+                k_turned[b, j] = k_sel[b, at, :].T
             return carry
 
         lax.fori_loop(0, count, prepare, 0)
-
-        def forward(b, carry):
+        for j in range(chunks):
+            slot_id = lax.broadcasted_iota(jnp.int32, (rows, LANES), 1)
+            of_row = j * (rows // KT) + lax.broadcasted_iota(jnp.int32, (rows, LANES), 0) // KT
+            onehot[j * rows : (j + 1) * rows, :] = jnp.where(slot_id == of_row, 1.0, 0.0).astype(
+                jnp.bfloat16
+            )
+
+        def forward(i, carry):
+            b = near_first(i)
             landed(1, q_all.at[block(b)], b)
-            bias = jnp.broadcast_to(bias_all[b][0:1, :], (rows, LANES))
+            bias = jnp.where(info_all[b][2:3, :] >= 0, 0.0, MASKED)
+            bias = jnp.broadcast_to(bias, (rows, LANES)).astype(jnp.bfloat16)
             query = jnp.concatenate([q_all[block(b), :], bias], axis=1)
             top = jnp.full((8, rows), MASKED, jnp.float32)
-            for j in range(count):
+            for j in range(chunks):
                 at = slice(j * rows, (j + 1) * rows)
-                key = jnp.concatenate([k_all[at, :], onehot[at, :]], axis=1)
+                key = jnp.concatenate([k_sel[b, at, :], onehot[at, :]], axis=1)
                 s = lax.dot_general(key, query, NT, preferred_element_type=jnp.float32)
                 scores[at, :] = s
                 top = jnp.maximum(top, jnp.max(s.reshape(rows // 8, 8, rows), axis=0))
             top = jnp.max(top, axis=0, keepdims=True)
             factor = scale * 1.4426950408889634
             summed = jnp.zeros((8, rows), jnp.float32)
-            for j in range(count):
+            for j in range(chunks):
                 at = slice(j * rows, (j + 1) * rows)
                 e = jnp.exp2((scores[at, :] - top) * factor)
                 weights[b, at, :] = e.astype(jnp.bfloat16)
@@ -200,71 +238,85 @@
             return carry
 
         lax.fori_loop(0, count, forward, 0)
-        dk_acc[...] = jnp.zeros_like(dk_acc)
-        dv_acc[...] = jnp.zeros_like(dv_acc)
 
         def values_in(b, carry):
-            landed(2, v_all.at[block(b)], b)
+            landed(2, v_all.at[tiles_of(b)], b)
             return carry
 
         lax.fori_loop(0, count, values_in, 0)
 
-        def backward(b, carry):
+        def pick_values(b, carry):
+            pick(v_all, v_sel, b)
+            return carry
+
+        lax.fori_loop(0, count, pick_values, 0)
+
+        def backward(i, carry):
+            b = near_first(i)
             landed(3, d_all.at[block(b)], b)
             d_b = d_all[block(b), :]
             q_b = q_all[block(b), :]
             inv = inverse[b][0:1, :]
             delta = jnp.zeros((8, rows), jnp.float32)
-            for j in range(count):
+            for j in range(chunks):
                 at = slice(j * rows, (j + 1) * rows)
-                dp = lax.dot_general(v_all[at, :], d_b, NT, preferred_element_type=jnp.float32)
+                dp = lax.dot_general(v_sel[b, at, :], d_b, NT, preferred_element_type=jnp.float32)
                 dprob[at, :] = dp
                 w = weights[b, at, :].astype(jnp.float32) * dp
                 delta = delta + jnp.sum(w.reshape(rows // 8, 8, rows), axis=0)
             delta = jnp.sum(delta, axis=0, keepdims=True) * inv
             dq = jnp.zeros((dim, rows), jnp.float32)
-            for j in range(count):
+            for j in range(chunks):
                 at = slice(j * rows, (j + 1) * rows)
                 p = weights[b, at, :].astype(jnp.float32) * inv
                 ds = (p * (dprob[at, :] - delta)).astype(jnp.bfloat16)
-                dv_acc[at, :] += jnp.dot(
-                    p.astype(jnp.bfloat16), d_b, preferred_element_type=jnp.float32
-                )
-                dk_acc[at, :] += jnp.dot(ds, q_b, preferred_element_type=jnp.float32)
-                dq = dq + jnp.dot(k_turned[j], ds, preferred_element_type=jnp.float32)
+                dv = jnp.dot(p.astype(jnp.bfloat16), d_b, preferred_element_type=jnp.float32)
+                dk = jnp.dot(ds, q_b, preferred_element_type=jnp.float32)
+                part = slice(j * tiles_here, (j + 1) * tiles_here)
+                dv_part[b, part] = dv.reshape(tiles_here, KT, dim)
+                dk_part[b, part] = dk.reshape(tiles_here, KT, dim)
+                dq = dq + jnp.dot(k_turned[b, j], ds, preferred_element_type=jnp.float32)
             dq_st[block(b), :] = (dq * scale).T.astype(jnp.bfloat16)
-            give(0, dq_st, dq_out, b)
-            return carry
-
-        def out_copy(kind, staged, out, b):
+            give(0, dq_st, b)
+            return carry
+
+        def out_copy(kind, staged, b):
             return pltpu.make_async_remote_copy(
                 src_ref=staged.at[block(b)],
-                dst_ref=out.at[head],
+                dst_ref=grads.at[kind, head],
                 send_sem=send_out.at[kind, b],
                 recv_sem=recv_out.at[kind, head],
                 device_id=(b, group),
                 device_id_type=MESH,
             )
 
-        def give(kind, staged, out, b):
+        def give(kind, staged, b):
             @pl.when(b != me)
             def _():
-                out_copy(kind, staged, out, b).start()
+                out_copy(kind, staged, b).start()
 
             @pl.when(b == me)
             def _():
                 pltpu.make_async_copy(
-                    staged.at[block(b)], out.at[head], recv_out.at[kind, head]
+                    staged.at[block(b)], grads.at[kind, head], recv_out.at[kind, head]
                 ).start()
 
         lax.fori_loop(0, count, backward, 0)
 
         def finish(i, carry):
-            b = (me + count // 2 + i) % count
-            dk_st[block(b), :] = (dk_acc[block(b), :] * scale).astype(jnp.bfloat16)
-            give(1, dk_st, dk_out, b)
-            dv_st[block(b), :] = dv_acc[block(b), :].astype(jnp.bfloat16)
-            give(2, dv_st, dv_out, b)
+            b = near_first(count - 1 - i)
+            for t in range(tiles_here):
+                dk = jnp.zeros((KT, dim), jnp.float32)
+                dv = jnp.zeros((KT, dim), jnp.float32)
+                for c in range(count):
+                    slot = info[c, 1, b * tiles_here + t]
+                    dk = dk + dk_part[c, slot]
+                    dv = dv + dv_part[c, slot]
+                at = pl.ds(pl.multiple_of(b * rows + t * KT, KT), KT)
+                dk_st[at, :] = (dk * scale).astype(jnp.bfloat16)
+                dv_st[at, :] = dv.astype(jnp.bfloat16)
+            give(1, dk_st, b)
+            give(2, dv_st, b)
             return carry
 
         lax.fori_loop(0, count, finish, 0)
@@ -272,8 +324,8 @@
         def sent(b, carry):
             @pl.when(b != me)
             def _():
-                for kind, staged, out in ((0, dq_st, dq_out), (1, dk_st, dk_out), (2, dv_st, dv_out)):
-                    out_copy(kind, staged, out, b).wait_send()
+                for kind, staged in ((0, dq_st), (1, dk_st), (2, dv_st)):
+                    out_copy(kind, staged, b).wait_send()
 
             return carry
 
@@ -286,16 +338,16 @@
 
         @pl.when(owner != me)
         def _():
-            in_copy(0, k_in.at[h], k_all.at[here], h, owner).wait_send()
+            in_copy(0, k_in.at[h], k_all.at[own_tiles], h, owner).wait_send()
             in_copy(1, q_in.at[h], q_all.at[here], h, owner).wait_send()
-            in_copy(2, v_in.at[h], v_all.at[here], h, owner).wait_send()
+            in_copy(2, v_in.at[h], v_all.at[own_tiles], h, owner).wait_send()
             in_copy(3, d_own.at[h], d_all.at[here], h, owner).wait_send()
-            in_copy(4, bias_own, bias_all.at[me], h, owner).wait_send()
-
-        for kind, out in ((0, dq_out), (1, dk_out), (2, dv_out)):
+            in_copy(4, info_own, info_all.at[me], h, owner).wait_send()
+
+        for kind in range(3):
             pltpu.make_async_remote_copy(
-                src_ref=out.at[h],
-                dst_ref=out.at[h],
+                src_ref=grads.at[kind, h],
+                dst_ref=grads.at[kind, h],
                 send_sem=send_out.at[kind, 0],
                 recv_sem=recv_out.at[kind, h],
                 device_id=((me + 1) % count, group),
@@ -309,37 +361,43 @@
     groups = lax.axis_size("head")
     total = count * rows
     width = grad_out.shape[1]
+    tiles_here = rows // KT
+    chosen = ((tiles_here + 2 + crit.shape[1]) // tiles_here + 1) * rows
     bf16, f32 = jnp.bfloat16, jnp.float32
-    anywhere = pl.BlockSpec(memory_space=pl.ANY)
+    hbm = pl.BlockSpec(memory_space=pl.ANY)
     vmem, dma = pltpu.VMEM, pltpu.SemaphoreType.DMA
-    out = jax.ShapeDtypeStruct((heads, rows, dim), bf16)
+    out = jax.ShapeDtypeStruct((3, heads, rows, dim), bf16)
     grads = pl.pallas_call(
         functools.partial(by_head_kernel, count, groups, crit.shape[1]),
-        out_shape=(out, out, out),
-        in_specs=[pl.BlockSpec(memory_space=pltpu.SMEM)] + [anywhere] * 5,
-        out_specs=(anywhere, anywhere, anywhere),
+        out_shape=out,
+        in_specs=[pl.BlockSpec(memory_space=pltpu.SMEM)] + [hbm] * 5,
+        out_specs=hbm,
         scratch_shapes=[
             vmem((total, dim), bf16),
+            vmem((total // KT, KT, dim), bf16),
+            vmem((total // KT, KT, dim), bf16),
             vmem((total, dim), bf16),
-            vmem((total, dim), bf16),
-            vmem((total, dim), bf16),
-            vmem((KT, LANES), bf16),
-            vmem((count, KT, LANES), bf16),
+            vmem((8, LANES), jnp.int32),
+            vmem((count, 8, LANES), jnp.int32),
+            pltpu.SMEM((count, 8, LANES), jnp.int32),
             vmem((groups, rows, width), bf16),
             vmem((groups, w_out.shape[0], width), bf16),
             vmem((rows, heads * dim), f32),
             vmem((heads, rows, dim), bf16),
-            vmem((total, LANES), bf16),
-            vmem((count, dim, rows), bf16),
-            vmem((count, total, rows), bf16),
-            vmem((total, rows), f32),
-            vmem((total, rows), f32),
+            vmem((chosen, LANES), bf16),
+            vmem((count, chosen, dim), bf16),
+            vmem((count, chosen // rows, dim, rows), bf16),
+            vmem((count, chosen, dim), bf16),
+            vmem((count, chosen, rows), bf16),
+            vmem((chosen, rows), f32),
+            vmem((chosen, rows), f32),
             vmem((count, 8, rows), f32),
-            vmem((total, dim), f32),
-            vmem((total, dim), f32),
+            vmem((count, chosen // KT, KT, dim), f32),
+            vmem((count, chosen // KT, KT, dim), f32),
             vmem((total, dim), bf16),
             vmem((total, dim), bf16),
             vmem((total, dim), bf16),
+            dma,
             dma((5, heads)),
             dma((5, count)),
             dma((groups,)),
@@ -349,17 +407,17 @@
             dma((3, heads)),
         ],
         compiler_params=pltpu.CompilerParams(
-            collective_id=0, has_side_effects=True, vmem_limit_bytes=52 * 2**20
+            collective_id=0, has_side_effects=True, vmem_limit_bytes=63 * 2**20 + 2**19
         ),
     )(
         crit,
         jnp.transpose(queries, (1, 0, 2)),
-        jnp.transpose(keys, (1, 0, 2)),
-        jnp.transpose(values, (1, 0, 2)),
+        jnp.transpose(keys, (1, 0, 2)).reshape(heads, tiles_here, KT, dim),
+        jnp.transpose(values, (1, 0, 2)).reshape(heads, tiles_here, KT, dim),
         grad_out,
         w_out,
     )
-    return tuple(jnp.transpose(grad, (1, 0, 2)) for grad in grads)
+    return tuple(jnp.transpose(grads[kind], (1, 0, 2)) for kind in range(3))
 
 
 def padded(cells, sides, width):
@@ -391,7 +449,7 @@
     count = lax.axis_size("tok")
     place = lax.axis_index("tok")
     tiles_here = tok_rows // KT
-    if heads_here <= count <= 2 * heads_here and count * tiles_here <= LANES:
+    if lax.axis_size("head") == 4 and heads_here <= count <= 2 * heads_here and count * tiles_here <= LANES and tok_rows % KT == 0 and tiles_here + crit.shape[1] < 110:
         return by_head(queries, keys, values, grad_out, w_out, crit)
     ncrit = crit.shape[1]
     capacity = (ncrit + count - 4) // (count - 3)

time: 77.4 us -> 72.2 us (0.933)
  the two profiles are of different devices: /device:TPU:24 before, /device:TPU:12 now
where the time goes in v2:
time: 72.2 us; the launch traced here: 72 us
  Pallas kernels  69.1 us (96%)
  local copies, waits for them, and re-layouts  2.26 us (3%)
    pallas_call x1, Pallas kernels, by_head(): pl.pallas_call(functools.partial(by_head_kernel, count, groups, crit.shap...  69.1 us
    transpose x1, local copies, waits for them, and re-layouts, by_head(): return tuple((jnp.transpose(grads[kind], (1, 0, 2)) for kind in range(3)))  2.26 us

profile of v2, /device:TPU:12, one launch (start us, length us, event | category | flops | bytes accessed | tf_op | source)
XLA Modules:
  0.0 72.0 jit_solution(5772933156433146049)
XLA Ops:
  0.6 69.1 %shard_map.85 = bf16[3,6,256,128]{3,2,1,0:T(8,128)(2,1)} custom-call(s32[1,40]{1,0:T(1,128)} %crit.1, bf16[6,256,128]{2,1,0:T(8,128)(2,1)} %bitcast.19, bf16[6,16,16,128]{3,2,1,0:T(8,128)(2,1)} %bitcast.20, bf16[6,16,16,128]{3,2,1,0:T(8,128)(2,1)} %bitcast.21, bf16[256,768]{1,0:T(8,128)(2,1)} %go_in.1, bf16[768,3072]{1,0:T(8,128)(2,1)} %w_in.1), custom_call_target="tpu_custom_call" | custom-call | tf_op jit(solution)/shard_map/pallas_call | solution.py:370
  69.8 2.3 %slice_bitcast_fusion = (bf16[256,6,128]{2,0,1:T(8,128)(2,1)}, bf16[256,6,128]{2,0,1:T(8,128)(2,1)}, bf16[256,6,128]{2,0,1:T(8,128)(2,1)}) fusion(bf16[3,6,256,128]{3,2,1,0:T(8,128)(2,1)} %shard_map.85), kind=kLoop, calls=%fused_computation | loop fusion | bytes 2359296 | tf_op jit(solution)/shard_map/transpose | solution.py:420

commit v3 on v2

--- a/solution.py
+++ b/solution.py
@@ -355,6 +355,27 @@
             ).wait_recv()
 
 
+def split_kernel(grads, dq_out, dk_out, dv_out, held, sems):
+    heads = grads.shape[1]
+    pieces = [(kind, h) for kind in range(3) for h in range(heads)]
+    outs = (dq_out, dk_out, dv_out)
+    fetches = [
+        pltpu.make_async_copy(grads.at[kind, h], held.at[kind, h], sems.at[0, kind, h])
+        for kind, h in pieces
+    ]
+    stores = [
+        pltpu.make_async_copy(held.at[kind, h], outs[kind].at[h], sems.at[1, kind, h])
+        for kind, h in pieces
+    ]
+    for fetch in fetches:
+        fetch.start()
+    for fetch, store in zip(fetches, stores):
+        fetch.wait()
+        store.start()
+    for store in stores:
+        store.wait()
+
+
 def by_head(queries, keys, values, grad_out, w_out, crit):
     rows, heads, dim = queries.shape
     count = lax.axis_size("tok")
@@ -364,14 +385,14 @@
     tiles_here = rows // KT
     chosen = ((tiles_here + 2 + crit.shape[1]) // tiles_here + 1) * rows
     bf16, f32 = jnp.bfloat16, jnp.float32
-    hbm = pl.BlockSpec(memory_space=pl.ANY)
+    anywhere = pl.BlockSpec(memory_space=pl.ANY)
     vmem, dma = pltpu.VMEM, pltpu.SemaphoreType.DMA
     out = jax.ShapeDtypeStruct((3, heads, rows, dim), bf16)
     grads = pl.pallas_call(
         functools.partial(by_head_kernel, count, groups, crit.shape[1]),
         out_shape=out,
-        in_specs=[pl.BlockSpec(memory_space=pltpu.SMEM)] + [hbm] * 5,
-        out_specs=hbm,
+        in_specs=[pl.BlockSpec(memory_space=pltpu.SMEM)] + [anywhere] * 5,
+        out_specs=anywhere,
         scratch_shapes=[
             vmem((total, dim), bf16),
             vmem((total // KT, KT, dim), bf16),
@@ -417,7 +438,16 @@
         grad_out,
         w_out,
     )
-    return tuple(jnp.transpose(grads[kind], (1, 0, 2)) for kind in range(3))
+    one = jax.ShapeDtypeStruct((heads, rows, dim), bf16)
+    grads = pl.pallas_call(
+        split_kernel,
+        out_shape=(one, one, one),
+        in_specs=[anywhere],
+        out_specs=(anywhere, anywhere, anywhere),
+        scratch_shapes=[vmem((3, heads, rows, dim), bf16), dma((2, 3, heads))],
+        compiler_params=pltpu.CompilerParams(vmem_limit_bytes=63 * 2**20 + 2**19),
+    )(grads)
+    return tuple(jnp.transpose(grad, (1, 0, 2)) for grad in grads)
 
 
 def padded(cells, sides, width):

time: 72.2 us -> 72.2 us (level)
  Pallas kernels: 69.1 us -> 71.4 us
  local copies, waits for them, and re-layouts: 2.26 us -> 0 us
    transpose x1 -> x0, local copies, waits for them, and re-layouts: 2.26 us -> none  [by_head(): return tuple((jnp.transpose(grads[kind], (1, 0, 2)) for kind in range(3)))]
    pallas_call x0 -> x1, Pallas kernels: none -> 2.23 us  [by_head(): pl.pallas_call(split_kernel, out_shape=(one, one, one), in_specs=[anywher...]
where the time goes in v3:
time: 72.2 us; the launch traced here: 72 us
  Pallas kernels  71.4 us (99%)
    pallas_call x1, Pallas kernels, by_head(): pl.pallas_call(functools.partial(by_head_kernel, count, groups, crit.shap...  69.1 us
    pallas_call x1, Pallas kernels, by_head(): pl.pallas_call(split_kernel, out_shape=(one, one, one), in_specs=[anywher...  2.23 us

profile of v3, /device:TPU:12, one launch (start us, length us, event | category | flops | bytes accessed | tf_op | source)
XLA Modules:
  0.0 72.0 jit_solution(9259853225334605133)
XLA Ops:
  0.6 69.1 %shard_map.85.grads = bf16[3,6,256,128]{3,2,1,0:T(8,128)(2,1)} custom-call(s32[1,40]{1,0:T(1,128)} %crit.1, bf16[6,256,128]{2,1,0:T(8,128)(2,1)} %bitcast.10, bf16[6,16,16,128]{3,2,1,0:T(8,128)(2,1)} %bitcast.11, bf16[6,16,16,128]{3,2,1,0:T(8,128)(2,1)} %bitcast.12, bf16[256,768]{1,0:T(8,128)(2,1)} %go_in.1, bf16[768,3072]{1,0:T(8,128)(2,1)} %w_in.1), custom_call_target="tpu_custom_call" | custom-call | tf_op jit(solution)/shard_map/pallas_call | solution.py:391
  69.8 2.2 %shard_map.86 = (bf16[6,256,128]{2,1,0:T(8,128)(2,1)}, bf16[6,256,128]{2,1,0:T(8,128)(2,1)}, bf16[6,256,128]{2,1,0:T(8,128)(2,1)}) custom-call(bf16[3,6,256,128]{3,2,1,0:T(8,128)(2,1)} %shard_map.85.grads), custom_call_target="tpu_custom_call" | custom-call | tf_op jit(solution)/shard_map/pallas_call | solution.py:442

commit v4 on v2

--- a/solution.py
+++ b/solution.py
@@ -16,21 +16,18 @@
 
 def owner_of(h, group, count, heads):
     gap = count - heads
-    odd = group % 2
-    late = jnp.where(h >= heads // 2, gap, 0)
-    return h + jnp.where(odd == 1, late, gap // 2)
+    spread = jnp.where(h == 0, 0, jnp.where(h == heads - 1, gap, gap // 2))
+    return h + jnp.where(group % 2 == 1, spread, gap // 2)
 
 
 def head_of(me, group, count, heads):
     gap = count - heads
-    half = heads // 2
-    odd = group % 2
-    even_head = me - gap // 2
-    odd_head = jnp.where(me < half, me, me - gap)
-    even_owns = (even_head >= 0) & (even_head < heads)
-    odd_owns = (me < half) | (me >= half + gap)
-    owns = ((odd == 1) & odd_owns) | ((odd == 0) & even_owns)
-    head = jnp.where(odd == 1, odd_head, even_head)
+    odd = group % 2 == 1
+    head = me - gap // 2
+    inner = jnp.where(odd, 1, 0)
+    owns = (head >= inner) & (head < heads - inner)
+    head = jnp.where(odd & (me == 0), 0, jnp.where(odd & (me == count - 1), heads - 1, head))
+    owns = owns | (odd & ((me == 0) | (me == count - 1)))
     return jnp.clip(head, 0, heads - 1), owns
 
 
@@ -179,7 +176,8 @@
     low = me < count // 2
 
     def near_first(i):
-        return jnp.where(low, i, count - 1 - i)
+        b = jnp.where(low, i, count - 1 - i)
+        return b + ((me + group) % 2) * (1 - 2 * (b % 2))
 
     @pl.when(owns)
     def _():
@@ -449,7 +447,7 @@
     count = lax.axis_size("tok")
     place = lax.axis_index("tok")
     tiles_here = tok_rows // KT
-    if lax.axis_size("head") == 4 and heads_here <= count <= 2 * heads_here and count * tiles_here <= LANES and tok_rows % KT == 0 and tiles_here + crit.shape[1] < 110:
+    if lax.axis_size("head") == 4 and count % 2 == 0 and 2 < heads_here <= count <= 2 * heads_here and count * tiles_here <= LANES and tok_rows % KT == 0 and tiles_here + crit.shape[1] < 110:
         return by_head(queries, keys, values, grad_out, w_out, crit)
     ncrit = crit.shape[1]
     capacity = (ncrit + count - 4) // (count - 3)

time: 72.2 us -> 72.3 us (level)
  the two profiles are of different devices: /device:TPU:12 before, /device:TPU:8 now
where the time goes in v4:
time: 72.3 us; the launch traced here: 72.1 us
  Pallas kernels  69.2 us (96%)
  local copies, waits for them, and re-layouts  2.26 us (3%)
    pallas_call x1, Pallas kernels, by_head(): pl.pallas_call(functools.partial(by_head_kernel, count, groups, crit.shap...  69.2 us
    transpose x1, local copies, waits for them, and re-layouts, by_head(): return tuple((jnp.transpose(grads[kind], (1, 0, 2)) for kind in range(3)))  2.26 us

profile of v4, /device:TPU:8, one launch (start us, length us, event | category | flops | bytes accessed | tf_op | source)
XLA Modules:
  0.0 72.1 jit_solution(15207498185414579107)
XLA Ops:
  0.6 69.2 %shard_map.85 = bf16[3,6,256,128]{3,2,1,0:T(8,128)(2,1)} custom-call(s32[1,40]{1,0:T(1,128)} %crit.1, bf16[6,256,128]{2,1,0:T(8,128)(2,1)} %bitcast.19, bf16[6,16,16,128]{3,2,1,0:T(8,128)(2,1)} %bitcast.20, bf16[6,16,16,128]{3,2,1,0:T(8,128)(2,1)} %bitcast.21, bf16[256,768]{1,0:T(8,128)(2,1)} %go_in.1, bf16[768,3072]{1,0:T(8,128)(2,1)} %w_in.1), custom_call_target="tpu_custom_call" | custom-call | tf_op jit(solution)/shard_map/pallas_call | solution.py:368
  69.8 2.3 %slice_bitcast_fusion = (bf16[256,6,128]{2,0,1:T(8,128)(2,1)}, bf16[256,6,128]{2,0,1:T(8,128)(2,1)}, bf16[256,6,128]{2,0,1:T(8,128)(2,1)}) fusion(bf16[3,6,256,128]{3,2,1,0:T(8,128)(2,1)} %shard_map.85), kind=kLoop, calls=%fused_computation | loop fusion | bytes 2359296 | tf_op jit(solution)/shard_map/transpose | solution.py:418

commit v5 on v4

--- a/solution.py
+++ b/solution.py
@@ -250,7 +250,7 @@
         lax.fori_loop(0, count, pick_values, 0)
 
         def backward(i, carry):
-            b = near_first(i)
+            b = near_first((i + count // 2) % count)
             landed(3, d_all.at[block(b)], b)
             d_b = d_all[block(b), :]
             q_b = q_all[block(b), :]

time: 72.3 us -> 71.8 us (level)
  the two profiles are of different devices: /device:TPU:8 before, /device:TPU:12 now
where the time goes in v5:
time: 71.8 us; the launch traced here: 70.3 us
  Pallas kernels  67.4 us (94%)
  local copies, waits for them, and re-layouts  2.26 us (3%)
    pallas_call x1, Pallas kernels, by_head(): pl.pallas_call(functools.partial(by_head_kernel, count, groups, crit.shap...  67.4 us
    transpose x1, local copies, waits for them, and re-layouts, by_head(): return tuple((jnp.transpose(grads[kind], (1, 0, 2)) for kind in range(3)))  2.26 us

profile of v5, /device:TPU:12, one launch (start us, length us, event | category | flops | bytes accessed | tf_op | source)
XLA Modules:
  0.0 70.3 jit_solution(12917777235139248969)
XLA Ops:
  0.6 67.4 %shard_map.85 = bf16[3,6,256,128]{3,2,1,0:T(8,128)(2,1)} custom-call(s32[1,40]{1,0:T(1,128)} %crit.1, bf16[6,256,128]{2,1,0:T(8,128)(2,1)} %bitcast.19, bf16[6,16,16,128]{3,2,1,0:T(8,128)(2,1)} %bitcast.20, bf16[6,16,16,128]{3,2,1,0:T(8,128)(2,1)} %bitcast.21, bf16[256,768]{1,0:T(8,128)(2,1)} %go_in.1, bf16[768,3072]{1,0:T(8,128)(2,1)} %w_in.1), custom_call_target="tpu_custom_call" | custom-call | tf_op jit(solution)/shard_map/pallas_call | solution.py:368
  68.1 2.3 %slice_bitcast_fusion = (bf16[256,6,128]{2,0,1:T(8,128)(2,1)}, bf16[256,6,128]{2,0,1:T(8,128)(2,1)}, bf16[256,6,128]{2,0,1:T(8,128)(2,1)}) fusion(bf16[3,6,256,128]{3,2,1,0:T(8,128)(2,1)} %shard_map.85), kind=kLoop, calls=%fused_computation | loop fusion | bytes 2359296 | tf_op jit(solution)/shard_map/transpose | solution.py:418
